TPU v7x, 512 devices: a whole 4x8x8 slice. The times are simulated.
512 devices in a mesh: section: 32 (over z, x), leaf: 16 (over y, core).
Axes of the slice: x: 4, y: 8, z: 8, core: 2. Of those that a mesh axis runs over, the one named last changes fastest.
Arguments:
- query_feats: bfloat16 [65536, 300], P(('section', 'leaf')), may hold values from -6 to 6
- query_weight: float32 [65536], P('section'), may hold values from 0.02 to 0.2
- positive_label: int32 [65536, 8], P('section'), may hold values from 0 to 131071, as said below
- positive_bucket: int32 [65536, 8], P('section'), may hold values from 0 to 15
- inv_prop: float32 [16], replicated, may hold values from 1 to 10
- primary_w: bfloat16 [131072, 300], P(('section', 'leaf')), may hold values from -0.375 to 0.375
- copy_owner: int32 [131072], P(('section', 'leaf')), may hold values from 0 to 31, as said below
- copy_row: int32 [131072], P(('section', 'leaf')), may hold values from 0 to 255
Outputs:
- query_grad: float32 [65536, 300], P(('section', 'leaf'))
- primary_grad: float32 [131072, 300], P(('section', 'leaf'))
Inputs may be any that keep to these rules, and one draw needn't show every extreme that they name: `copy_owner`: each copy names a section other than its own device's; among the copies of one device at most 16 name one owner, and exactly 16 name one of them. `positive_label`: every listed label is the label of some slot, primary or copy, of the query's own section; a label may be listed twice.
All inputs are finite; a program needn't handle non-finite values.
Results may differ from a plain program's by a relative error of at most 0.0018.
Values may be sent and summed in bfloat16 or wider, within the bound.
No kernel may reach another device: no remote copies, remote signals or barrier semaphores. Data moves between devices by JAX's collectives and lax.ppermute only.
A program may use at most 64 MiB of HBM per device.

v0:
```python
import math
import jax
import jax.numpy as jnp
from jax import lax
from jax.sharding import PartitionSpec as P


def on_device(
    query_feats,
    query_weight,
    positive_label,
    positive_bucket,
    inv_prop,
    primary_w,
    copy_owner,
    copy_row,
):
    sections = lax.axis_size("section")
    leaves = lax.axis_size("leaf")
    section_id = lax.axis_index("section")
    leaf_id = lax.axis_index("leaf")
    prim_rows = primary_w.shape[0]
    copy_count = copy_owner.shape[0]
    feature_dim = primary_w.shape[1]
    capacity = 8 * ((2 * copy_count // (sections - 1) + 7) // 8)
    owner_hot = (copy_owner[:, None] == jnp.arange(sections, dtype=jnp.int32)[None, :]).astype(
        jnp.float32
    )
    before = jnp.cumsum(owner_hot, axis=0) - owner_hot
    rank_in = jnp.sum(before * owner_hot, axis=1).astype(jnp.int32)
    target = copy_owner * capacity + rank_in
    requests = (
        jnp.zeros((sections * capacity,), jnp.int32)
        .at[target]
        .set(copy_row)
        .reshape(sections, capacity)
    )
    wanted = lax.all_to_all(requests, "section", split_axis=0, concat_axis=0, tiled=True)
    served = jnp.take(primary_w, wanted.reshape(-1), axis=0).reshape(
        sections, capacity, feature_dim
    )
    arrived = lax.all_to_all(served, "section", split_axis=0, concat_axis=0, tiled=True)
    copy_w = jnp.take(arrived.reshape(sections * capacity, feature_dim), target, axis=0)
    weights = jnp.concatenate([primary_w, copy_w], axis=0)
    first_label = (section_id * leaves + leaf_id) * prim_rows
    labels = jnp.concatenate(
        [
            first_label + jnp.arange(prim_rows, dtype=jnp.int32),
            (copy_owner * leaves + leaf_id) * prim_rows + copy_row,
        ]
    )
    bucket_hot = positive_bucket[..., None] == jnp.arange(inv_prop.shape[0], dtype=jnp.int32)
    pos_value = jnp.sum(jnp.where(bucket_hot, inv_prop, 0.0), axis=-1)
    slot_count = weights.shape[0]
    section_rows = positive_label.shape[0]
    start_state = (
        jnp.zeros((slot_count, feature_dim), jnp.float32),
        jnp.zeros((section_rows, feature_dim), jnp.float32),
    )
    shard_rows = lax.all_gather(query_feats, "leaf", axis=0, tiled=True)
    piece_rows = shard_rows.shape[0]
    block_rows = math.gcd(piece_rows, 256)

    def block_step(block_num, partial_sums):
        slot_acc, query_acc = partial_sums
        offset_row = block_num * block_rows
        q_block = lax.dynamic_slice_in_dim(shard_rows, offset_row, block_rows, 0)
        labels_block = lax.dynamic_slice_in_dim(positive_label, offset_row, block_rows, 0)
        values_block = lax.dynamic_slice_in_dim(pos_value, offset_row, block_rows, 0)
        scale_block = lax.dynamic_slice_in_dim(query_weight, offset_row, block_rows, 0)
        logits = lax.dot_general(
            q_block, weights, (((1,), (1,)), ((), ())), preferred_element_type=jnp.float32
        )
        sigmoid_val = jax.nn.sigmoid(logits)
        hit_count = jnp.zeros(logits.shape, jnp.float32)
        pos_weight = jnp.zeros(logits.shape, jnp.float32)
        for column in range(labels_block.shape[1]):
            matched = (labels[None, :] == labels_block[:, column : column + 1]).astype(jnp.float32)
            hit_count = hit_count + matched
            pos_weight = pos_weight + matched * values_block[:, column : column + 1]
        mixed = (1.0 - jnp.minimum(hit_count, 1.0)) * sigmoid_val + pos_weight * (sigmoid_val - 1.0)
        coefficient = (scale_block[:, None] * mixed).astype(jnp.bfloat16)
        query_part = jnp.dot(coefficient, weights, preferred_element_type=jnp.float32)
        query_acc = lax.dynamic_update_slice_in_dim(query_acc, query_part, offset_row, 0)
        slot_acc = slot_acc + lax.dot_general(
            coefficient, q_block, (((0,), (0,)), ((), ())), preferred_element_type=jnp.float32
        )
        return (slot_acc, query_acc)

    slot_grad, query_sum = lax.fori_loop(0, piece_rows // block_rows, block_step, start_state)
    send_back = (
        jnp.zeros((sections * capacity, feature_dim), jnp.float32)
        .at[target]
        .set(slot_grad[prim_rows:])
        .reshape(sections, capacity, feature_dim)
    )
    returned = lax.all_to_all(send_back, "section", split_axis=0, concat_axis=0, tiled=True)
    primary_grad = (
        slot_grad[:prim_rows].at[wanted.reshape(-1)].add(returned.reshape(-1, feature_dim))
    )
    query_whole = lax.psum(query_sum, "leaf")
    query_grad = lax.dynamic_slice_in_dim(
        query_whole, leaf_id * query_feats.shape[0], query_feats.shape[0], 0
    )
    return (query_grad, primary_grad)


def solution(mesh):
    placed = (
        P(("section", "leaf"), None),
        P("section"),
        P("section", None),
        P("section", None),
        P(),
        P(("section", "leaf"), None),
        P(("section", "leaf")),
        P(("section", "leaf")),
    )
    return jax.shard_map(
        on_device,
        mesh=mesh,
        in_specs=placed,
        out_specs=(P(("section", "leaf"), None), P(("section", "leaf"), None)),
        check_vma=False,
    )
```

profile of v0, /device:TPU:1, one launch (start us, length us, event | category | flops | bytes accessed | tf_op | source)
XLA Modules:
  0.0 241.0 jit_solution(1173304423045071907)
XLA Ops:
  7.2 1.6 copy.31
  11.8 1.6 scatter_custom_fusion
  14.0 13.7 %all-to-all-start = ((s32[32,1,16]{2,1,0:T(1,128)}), s32[32,1,16]{2,1,0:T(1,128)S(1)}, u32[]{:S(2)}, u32[]{:S(2)}) async-start(s32[32,1,16]{2,1,0:T(1,128)} %bitcast.2), calls=%async_computation | async-start | bytes 32768 | tf_op jit(solution)/shard_map/all_to_all | solution.py:38
  27.8 1.1 copy.35
  28.9 7.4 %all-to-all-done = s32[32,1,16]{2,1,0:T(1,128)S(1)} async-done(((s32[32,1,16]{2,1,0:T(1,128)}), s32[32,1,16]{2,1,0:T(1,128)S(1)}, u32[]{:S(2)}, u32[]{:S(2)}) %all-to-all-start) | async-done | bytes 2080 | tf_op jit(solution)/shard_map/all_to_all | solution.py:38
  37.6 1.9 gather_fusion
  40.5 3.9 %all-to-all-start.1 = ((bf16[32,16,300]{2,1,0:T(8,128)(2,1)}), bf16[32,16,300]{2,1,0:T(8,128)(2,1)S(1)}, u32[]{:S(2)}, u32[]{:S(2)}) async-start(bf16[32,16,300]{2,1,0:T(8,128)(2,1)} %broadcast_select_fusion), calls=%async_computation.1 | async-start | bytes 786432 | tf_op jit(solution)/shard_map/all_to_all | solution.py:42
  45.4 10.8 %all-to-all-done.1 = bf16[32,16,300]{2,1,0:T(8,128)(2,1)S(1)} async-done(((bf16[32,16,300]{2,1,0:T(8,128)(2,1)}), bf16[32,16,300]{2,1,0:T(8,128)(2,1)S(1)}, u32[]{:S(2)}, u32[]{:S(2)}) %all-to-all-start.1) | async-done | bytes 307232 | tf_op jit(solution)/shard_map/all_to_all | solution.py:42
  56.3 1.2 gather_fusion.1
  58.3 51.9 %while.18 = (s32[]{:T(128)}, f32[512,300]{0,1:T(8,128)S(1)}, f32[2048,300]{0,1:T(8,128)S(1)}, f32[2048]{0:T(1024)}, s32[512]{0:T(512)S(1)}, /*index=5*/s32[2048,...) while((s32[]{:T(128)}, f32[512,300]{0,1:T(8,128)S(1)}, ...), condition=%wide.region_6.7_spmd.clone, body=%wide.region_5.6_spmd.clone.sunk | while | flops 242659344 | bytes 3474841 | solution.py:90
  59.1 1.1 constant_dynamic-slice_fusion.5
  60.2 1.1 constant_dynamic-slice_fusion.6
  61.3 2.0 fusion.53
  63.2 1.2 convolution_add_fusion.2
  65.6 1.1 constant_dynamic-slice_fusion.5
  66.7 1.1 constant_dynamic-slice_fusion.6
  67.8 2.0 fusion.53
  69.7 1.2 convolution_add_fusion.2
  72.1 1.1 constant_dynamic-slice_fusion.5
  73.1 1.1 constant_dynamic-slice_fusion.6
  74.2 2.0 fusion.53
  76.2 1.2 convolution_add_fusion.2
  78.6 1.1 constant_dynamic-slice_fusion.5
  79.6 1.1 constant_dynamic-slice_fusion.6
  80.7 2.0 fusion.53
  82.7 1.2 convolution_add_fusion.2
  85.0 1.1 constant_dynamic-slice_fusion.5
  86.1 1.1 constant_dynamic-slice_fusion.6
  87.2 2.0 fusion.53
  89.2 1.2 convolution_add_fusion.2
  91.5 1.1 constant_dynamic-slice_fusion.5
  92.6 1.1 constant_dynamic-slice_fusion.6
  93.7 2.0 fusion.53
  95.7 1.2 convolution_add_fusion.2
  98.0 1.1 constant_dynamic-slice_fusion.5
  99.1 1.1 constant_dynamic-slice_fusion.6
  100.2 2.0 fusion.53
  102.1 1.2 convolution_add_fusion.2
  105.6 1.1 constant_dynamic-slice_fusion.6
  106.7 2.0 fusion.53
  108.6 1.2 convolution_add_fusion.2
  110.2 1.4 copy-done
  111.9 2.3 scatter_custom_fusion.1
  114.2 10.0 %all-to-all-start.2 = ((f32[32,16,300]{2,1,0:T(8,128)}), f32[32,16,300]{2,1,0:T(8,128)S(1)}, u32[]{:S(2)}, u32[]{:S(2)}) async-start(f32[32,16,300]{2,1,0:T(8,128)} %bitcast.7), calls=%async_computation.2 | async-start | bytes 1572864 | tf_op jit(solution)/shard_map/all_to_all | solution.py:97
  124.5 21.2 %all-to-all-done.2 = f32[32,16,300]{2,1,0:T(8,128)S(1)} async-done(((f32[32,16,300]{2,1,0:T(8,128)}), f32[32,16,300]{2,1,0:T(8,128)S(1)}, u32[]{:S(2)}, u32[]{:S(2)}) %all-to-all-start.2) | async-done | bytes 614432 | tf_op jit(solution)/shard_map/all_to_all | solution.py:97
  145.7 3.8 %scatter_fusion = f32[256,300]{1,0:T(8,128)S(1)} fusion(f32[256,300]{1,0:T(8,128)S(1)} %slice.197, s32[512]{0:T(512)S(1)} %bitcast.110, f32[512,300]{1,0:T(8,128)S(1)} %bitcast.90), kind=kCustom, calls=%fused_computation.4 | custom fusion | flops 153600 | bytes 1845248 | tf_op jit(solution)/shard_map/scatter-add | solution.py:99
  150.3 82.2 %all-reduce.2.cloned.1.call-done = f32[2048,300]{0,1:T(8,128)} async-done(((f32[2048,300]{0,1:T(8,128)}), f32[2048,300]{0,1:T(8,128)}) %all-reduce.2.cloned.1.call-update) | async-done | bytes 2457616 | tf_op jit(solution)/shard_map/psum | solution.py:101
  232.5 1.6 constant_dynamic-slice_fusion.2
  (60 shorter events, 18.6 us)
Async XLA Ops:
  7.2 50.9 %all-gather.2.cloned.1.call-start = ((), (), s32[]{:S(2)}) async-start(), calls=%async_computation.3 | async-start | bytes 1671168 | tf_op jit(solution)/shard_map/all_gather | solution.py:60
  14.0 22.2 %all-to-all-start = ((s32[32,1,16]{2,1,0:T(1,128)}), s32[32,1,16]{2,1,0:T(1,128)S(1)}, u32[]{:S(2)}, u32[]{:S(2)}) async-start(s32[32,1,16]{2,1,0:T(1,128)} %bitcast.2), calls=%async_computation | async-start | bytes 32768 | tf_op jit(solution)/shard_map/all_to_all | solution.py:38
  37.6 6.9 %copy-start.2 = (s32[256]{0:T(256)S(1)}, s32[256]{0:T(256)}, u32[]{:S(2)}) copy-start(s32[256]{0:T(256)} %param.16) | copy-start | bytes 3076
  37.6 6.9 %copy-start.3 = (s32[256]{0:T(256)S(1)}, s32[256]{0:T(256)}, u32[]{:S(2)}) copy-start(s32[256]{0:T(256)} %param.17) | copy-start | bytes 3076
  37.6 6.9 %copy-start.1 = (s32[2048,8]{0,1:T(8,128)S(1)}, s32[2048,8]{0,1:T(8,128)}, u32[]{:S(2)}) copy-start(s32[2048,8]{0,1:T(8,128)} %param.13) | copy-start | bytes 196612
  37.6 6.9 %copy-start.4 = (f32[16]{0:T(128)S(1)}, f32[16]{0:T(128)}, u32[]{:S(2)}) copy-start(f32[16]{0:T(128)} %param.14) | copy-start | bytes 196
  40.5 15.8 %all-to-all-start.1 = ((bf16[32,16,300]{2,1,0:T(8,128)(2,1)}), bf16[32,16,300]{2,1,0:T(8,128)(2,1)S(1)}, u32[]{:S(2)}, u32[]{:S(2)}) async-start(bf16[32,16,300]{2,1,0:T(8,128)(2,1)} %broadcast_select_fusion), calls=%async_computation.1 | async-start | bytes 786432 | tf_op jit(solution)/shard_map/all_to_all | solution.py:42
  44.4 188.2 %all-reduce.2.cloned.1.call-start = ((), (), s32[]{:S(2)}) async-start(), calls=%async_computation.4 | async-start | bytes 4980736 | tf_op jit(solution)/shard_map/psum | solution.py:101
  110.2 1.5 copy-start
  114.2 31.5 %all-to-all-start.2 = ((f32[32,16,300]{2,1,0:T(8,128)}), f32[32,16,300]{2,1,0:T(8,128)S(1)}, u32[]{:S(2)}, u32[]{:S(2)}) async-start(f32[32,16,300]{2,1,0:T(8,128)} %bitcast.7), calls=%async_computation.2 | async-start | bytes 1572864 | tf_op jit(solution)/shard_map/all_to_all | solution.py:97
Sparse Core Ops, SparseCore 0:
  10.7 47.2 all-gather.1
  111.8 120.6 all-reduce.1
where the time goes:
time: 243 us; the launch traced here: 241 us
  waiting for transfers between devices  122 us (50%)
  local copies, waits for them, and re-layouts  39.2 us (16%)
  matrix products  28 us (12%)
  starting transfers between devices  27.7 us (11%)
  between operations  14.3 us (6%)
  other arithmetic  9.21 us (4%)
    psum x1, waiting for transfers between devices, on_device(): query_whole = lax.psum(query_sum, 'leaf')  82.2 us
    all_to_all x1, waiting for transfers between devices, on_device(): lax.all_to_all(send_back, 'section', split_axis=0, concat_axis=0, tiled=T...  21.2 us
    dot_general x8, matrix products, block_step(): lax.dot_general(q_block, weights, (((1,), (1,)), ((), ())), preferred_ele...  15.7 us
    all_to_all x1, starting transfers between devices, on_device(): lax.all_to_all(requests, 'section', split_axis=0, concat_axis=0, tiled=True)  13.7 us
    all_to_all x1, waiting for transfers between devices, on_device(): lax.all_to_all(served, 'section', split_axis=0, concat_axis=0, tiled=True)  10.8 us
    all_to_all x1, starting transfers between devices, on_device(): lax.all_to_all(send_back, 'section', split_axis=0, concat_axis=0, tiled=T...  10 us
    dot_general x8, matrix products, block_step(): lax.dot_general(coefficient, q_block, (((0,), (0,)), ((), ())), preferred...  10 us
    slice x8, local copies, waits for them, and re-layouts, block_step(): labels_block[:, column:column + 1]  8.72 us
  transfers between devices with their start and end apart: 5, of which 5 were waited for; matrix products, arithmetic and copies ran while one was open for 8% of the time, Pallas kernels for 0%

commit v1 on v0

--- a/solution.py
+++ b/solution.py
@@ -98,7 +98,7 @@
     primary_grad = (
         slot_grad[:prim_rows].at[wanted.reshape(-1)].add(returned.reshape(-1, feature_dim))
     )
-    query_whole = lax.psum(query_sum, "leaf")
+    query_whole = jnp.sum(lax.all_gather(query_sum, "leaf"), axis=0)
     query_grad = lax.dynamic_slice_in_dim(
         query_whole, leaf_id * query_feats.shape[0], query_feats.shape[0], 0
     )

time: 243 us -> 370 us (1.52)
  waiting for transfers between devices: 122 us -> 208 us
  local copies, waits for them, and re-layouts: 39.2 us -> 66.8 us
  other arithmetic: 9.21 us -> 17.1 us
  matrix products: 28 us -> 34 us
    all_gather x0 -> x1, waiting for transfers between devices: none -> 167 us  [on_device(): query_whole = jnp.sum(lax.all_gather(query_sum, 'leaf'), axis=0)]
    psum x1 -> x0, waiting for transfers between devices: 82.2 us -> none  [on_device(): query_whole = lax.psum(query_sum, 'leaf')]
    unnamed x13 -> x12, local copies, waits for them, and re-layouts: 5.05 us -> 38.8 us
    reduce_sum x0 -> x1, other arithmetic: none -> 8.38 us  [on_device(): query_whole = jnp.sum(lax.all_gather(query_sum, 'leaf'), axis=0)]
    slice x8, local copies, waits for them, and re-layouts: 8.56 us -> 0.75 us  [block_step(): pos_weight = pos_weight + matched * values_block[:, column:column + 1]]
    dot_general x8, matrix products: 2.36 us -> 8.47 us  [block_step(): jnp.dot(coefficient, weights, preferred_element_type=jnp.float32)]
  transfers between devices with their start and end apart: 5 -> 5, of which waited for: 5 -> 5; matrix products, arithmetic and copies ran while one was open for 8% -> 5% of each run, Pallas kernels for 0% -> 0%
where the time goes in v1:
time: 370 us; the launch traced here: 368 us
  waiting for transfers between devices  208 us (56%)
  local copies, waits for them, and re-layouts  66.8 us (18%)
  matrix products  34 us (9%)
  starting transfers between devices  27.7 us (7%)
  other arithmetic  17.1 us (5%)
  between operations  14.3 us (4%)
    all_gather x1, waiting for transfers between devices, on_device(): query_whole = jnp.sum(lax.all_gather(query_sum, 'leaf'), axis=0)  167 us
    unnamed x12, local copies, waits for them, and re-layouts  38.8 us
    all_to_all x1, waiting for transfers between devices, on_device(): lax.all_to_all(send_back, 'section', split_axis=0, concat_axis=0, tiled=T...  21.2 us
    dot_general x8, matrix products, block_step(): lax.dot_general(q_block, weights, (((1,), (1,)), ((), ())), preferred_ele...  15.6 us
    all_to_all x1, starting transfers between devices, on_device(): lax.all_to_all(requests, 'section', split_axis=0, concat_axis=0, tiled=True)  13.7 us
    all_to_all x1, waiting for transfers between devices, on_device(): lax.all_to_all(served, 'section', split_axis=0, concat_axis=0, tiled=True)  11.5 us
    all_to_all x1, starting transfers between devices, on_device(): lax.all_to_all(send_back, 'section', split_axis=0, concat_axis=0, tiled=T...  10 us
    dot_general x8, matrix products, block_step(): lax.dot_general(coefficient, q_block, (((0,), (0,)), ((), ())), preferred...  9.94 us
  transfers between devices with their start and end apart: 5, of which 5 were waited for; matrix products, arithmetic and copies ran while one was open for 5% of the time, Pallas kernels for 0%

profile of v1, /device:TPU:1, one launch (start us, length us, event | category | flops | bytes accessed | tf_op | source)
XLA Modules:
  0.0 367.9 jit_solution(5609811879122531863)
XLA Ops:
  7.2 1.6 copy.31
  11.8 1.6 scatter_custom_fusion
  14.0 13.7 %all-to-all-start = ((s32[32,1,16]{2,1,0:T(1,128)}), s32[32,1,16]{2,1,0:T(1,128)S(1)}, u32[]{:S(2)}, u32[]{:S(2)}) async-start(s32[32,1,16]{2,1,0:T(1,128)} %bitcast.2), calls=%async_computation | async-start | bytes 32768 | tf_op jit(solution)/shard_map/all_to_all | solution.py:38
  27.8 1.1 copy.35
  28.9 7.4 %all-to-all-done = s32[32,1,16]{2,1,0:T(1,128)S(1)} async-done(((s32[32,1,16]{2,1,0:T(1,128)}), s32[32,1,16]{2,1,0:T(1,128)S(1)}, u32[]{:S(2)}, u32[]{:S(2)}) %all-to-all-start) | async-done | bytes 2080 | tf_op jit(solution)/shard_map/all_to_all | solution.py:38
  37.6 1.9 gather_fusion
  40.5 3.9 %all-to-all-start.1 = ((bf16[32,16,300]{2,1,0:T(8,128)(2,1)}), bf16[32,16,300]{2,1,0:T(8,128)(2,1)S(1)}, u32[]{:S(2)}, u32[]{:S(2)}) async-start(bf16[32,16,300]{2,1,0:T(8,128)(2,1)} %broadcast_select_fusion), calls=%async_computation.1 | async-start | bytes 786432 | tf_op jit(solution)/shard_map/all_to_all | solution.py:42
  44.8 11.5 %all-to-all-done.1 = bf16[32,16,300]{2,1,0:T(8,128)(2,1)S(1)} async-done(((bf16[32,16,300]{2,1,0:T(8,128)(2,1)}), bf16[32,16,300]{2,1,0:T(8,128)(2,1)S(1)}, u32[]{:S(2)}, u32[]{:S(2)}) %all-to-all-start.1) | async-done | bytes 307232 | tf_op jit(solution)/shard_map/all_to_all | solution.py:42
  56.3 1.2 gather_fusion.1
  58.0 1.8 broadcast_in_dim.53
  59.8 50.1 %while.18 = (s32[]{:T(128)}, f32[512,300]{0,1:T(8,128)S(1)}, f32[2048,300]{0,1:T(8,128)}, f32[2048]{0:T(1024)}, s32[512]{0:T(512)S(1)}, /*index=5*/s32[2048,8]{0...) while((s32[]{:T(128)}, f32[512,300]{0,1:T(8,128)S(1)}, ...), condition=%wide.region_6.7_spmd.clone, body=%wide.region_5.6_spmd.clone.sunk | while | flops 242659344 | bytes 3388817 | solution.py:90
  59.9 1.1 constant_dynamic-slice_fusion.6
  61.8 1.9 fusion.53
  63.7 1.1 convolution_dynamic-update-slice_fusion.2
  64.8 1.2 convolution_add_fusion.2
  66.1 1.1 constant_dynamic-slice_fusion.6
  68.0 1.9 fusion.53
  70.0 1.1 convolution_dynamic-update-slice_fusion.2
  71.0 1.2 convolution_add_fusion.2
  72.4 1.3 constant_dynamic-slice_fusion.6
  74.4 1.9 fusion.53
  76.4 1.1 convolution_dynamic-update-slice_fusion.2
  77.5 1.2 convolution_add_fusion.2
  78.8 1.1 constant_dynamic-slice_fusion.6
  80.7 1.9 fusion.53
  83.7 1.2 convolution_add_fusion.2
  85.1 1.1 constant_dynamic-slice_fusion.6
  86.9 1.9 fusion.53
  88.9 1.1 convolution_dynamic-update-slice_fusion.2
  89.9 1.2 convolution_add_fusion.2
  91.3 1.1 constant_dynamic-slice_fusion.6
  93.2 1.9 fusion.53
  96.1 1.2 convolution_add_fusion.2
  97.5 1.1 constant_dynamic-slice_fusion.6
  99.4 1.9 fusion.53
  102.3 1.2 convolution_add_fusion.2
  103.7 1.1 constant_dynamic-slice_fusion.6
  105.6 1.9 fusion.53
  107.5 1.1 convolution_dynamic-update-slice_fusion.2
  108.6 1.2 convolution_add_fusion.2
  110.1 2.3 scatter_custom_fusion.1
  112.4 10.0 %all-to-all-start.2 = ((f32[32,16,300]{2,1,0:T(8,128)}), f32[32,16,300]{2,1,0:T(8,128)S(1)}, u32[]{:S(2)}, u32[]{:S(2)}) async-start(f32[32,16,300]{2,1,0:T(8,128)} %bitcast.7), calls=%async_computation.2 | async-start | bytes 1572864 | tf_op jit(solution)/shard_map/all_to_all | solution.py:97
  122.7 21.2 %all-to-all-done.2 = f32[32,16,300]{2,1,0:T(8,128)S(1)} async-done(((f32[32,16,300]{2,1,0:T(8,128)}), f32[32,16,300]{2,1,0:T(8,128)S(1)}, u32[]{:S(2)}, u32[]{:S(2)}) %all-to-all-start.2) | async-done | bytes 614432 | tf_op jit(solution)/shard_map/all_to_all | solution.py:97
  143.9 3.9 %scatter_fusion = f32[256,300]{1,0:T(8,128)S(1)} fusion(f32[256,300]{1,0:T(8,128)S(1)} %slice.197, s32[512]{0:T(512)S(1)} %bitcast.116, f32[512,300]{1,0:T(8,128)S(1)} %bitcast.96), kind=kCustom, calls=%fused_computation.4 | custom fusion | flops 153600 | bytes 1845248 | tf_op jit(solution)/shard_map/scatter-add | solution.py:99
  148.7 167.1 %all-gather.6.cloned.1.call-done = f32[32768,300]{0,1:T(8,128)} async-done(((f32[2048,300]{0,1:T(8,128)}), f32[32768,300]{0,1:T(8,128)}) %all-gather.6.cloned.1.call-update) | async-done | bytes 39321616 | tf_op jit(solution)/shard_map/all_gather | solution.py:101
  315.9 35.2 %copy.40 = f32[38,8,16,2048]{3,2,1,0:T(8,128)S(1)} copy(f32[38,8,16,2048]{3,1,2,0:T(8,128)} %bitcast.94) | data formatting | bytes 79691776
  351.1 8.4 %bitcast_reduce_fusion = f32[2048,300]{0,1:T(8,128)} fusion(f32[304,16,2048]{2,1,0:T(8,128)S(1)} %bitcast.93), kind=kLoop, calls=%fused_computation.54 | loop fusion | flops 9216000 | bytes 41779200 | tf_op jit(solution)/shard_map/reduce_sum | solution.py:101
  359.5 1.6 constant_dynamic-slice_fusion.2
  (60 shorter events, 18.2 us)
Async XLA Ops:
  7.2 50.9 %all-gather.4.cloned.1.call-start = ((), (), s32[]{:S(2)}) async-start(), calls=%async_computation.3 | async-start | bytes 1671168 | tf_op jit(solution)/shard_map/all_gather | solution.py:60
  14.0 22.2 %all-to-all-start = ((s32[32,1,16]{2,1,0:T(1,128)}), s32[32,1,16]{2,1,0:T(1,128)S(1)}, u32[]{:S(2)}, u32[]{:S(2)}) async-start(s32[32,1,16]{2,1,0:T(1,128)} %bitcast.2), calls=%async_computation | async-start | bytes 32768 | tf_op jit(solution)/shard_map/all_to_all | solution.py:38
  37.6 6.9 %copy-start.1 = (s32[256]{0:T(256)S(1)}, s32[256]{0:T(256)}, u32[]{:S(2)}) copy-start(s32[256]{0:T(256)} %param.16) | copy-start | bytes 3076
  37.6 6.9 %copy-start.2 = (s32[256]{0:T(256)S(1)}, s32[256]{0:T(256)}, u32[]{:S(2)}) copy-start(s32[256]{0:T(256)} %param.17) | copy-start | bytes 3076
  37.6 6.9 %copy-start = (s32[2048,8]{0,1:T(8,128)S(1)}, s32[2048,8]{0,1:T(8,128)}, u32[]{:S(2)}) copy-start(s32[2048,8]{0,1:T(8,128)} %param.13) | copy-start | bytes 196612
  37.6 6.9 %copy-start.3 = (f32[16]{0:T(128)S(1)}, f32[16]{0:T(128)}, u32[]{:S(2)}) copy-start(f32[16]{0:T(128)} %param.14) | copy-start | bytes 196
  40.5 15.8 %all-to-all-start.1 = ((bf16[32,16,300]{2,1,0:T(8,128)(2,1)}), bf16[32,16,300]{2,1,0:T(8,128)(2,1)S(1)}, u32[]{:S(2)}, u32[]{:S(2)}) async-start(bf16[32,16,300]{2,1,0:T(8,128)(2,1)} %broadcast_select_fusion), calls=%async_computation.1 | async-start | bytes 786432 | tf_op jit(solution)/shard_map/all_to_all | solution.py:42
  44.4 271.5 %all-gather.6.cloned.1.call-start = ((), (), s32[]{:S(2)}) async-start(), calls=%async_computation.4 | async-start | bytes 42336256 | tf_op jit(solution)/shard_map/all_gather | solution.py:101
  112.4 31.5 %all-to-all-start.2 = ((f32[32,16,300]{2,1,0:T(8,128)}), f32[32,16,300]{2,1,0:T(8,128)S(1)}, u32[]{:S(2)}, u32[]{:S(2)}) async-start(f32[32,16,300]{2,1,0:T(8,128)} %bitcast.7), calls=%async_computation.2 | async-start | bytes 1572864 | tf_op jit(solution)/shard_map/all_to_all | solution.py:97
Sparse Core Ops, SparseCore 0:
  10.7 47.2 all-gather.3
  110.0 205.7 all-gather.5
